TPU v7x, 32 devices: a whole 2x2x4 slice. The times are simulated.
32 devices in a mesh: groups: 2 (over x), dp: 16 (over z, y, core).
Axes of the slice: x: 2, y: 2, z: 4, core: 2. Of those that a mesh axis runs over, the one named last changes fastest.
Arguments:
- teacher_blocks: bfloat16 [24576, 2048], P(('groups', 'dp')), parts along dimension 0, may hold values from -9 to 9
- student_blocks: bfloat16 [24576, 2048], P(('groups', 'dp')), parts along dimension 0, may hold values from -9 to 9
- block_expert: int32 [192], P(('groups', 'dp')), parts along dimension 0, may hold values from 0 to 1
- block_count: int32 [32], P(('groups', 'dp')), parts along dimension 0, may hold values from 1 to 6, as said below
- gate_weight: bfloat16 [4, 2048, 384], P('groups'), parts along dimension 0, may hold values from -0.125 to 0.125
- up_weight: bfloat16 [4, 2048, 384], P('groups'), parts along dimension 0, may hold values from -0.125 to 0.125
Outputs:
- panels: float32 [1536, 768], P(('groups', 'dp')), parts along dimension 0
There are 2 independent parts, one for each index of `groups`. A program takes and returns all parts, laid end to end along the dimension named above; each array names one. Nothing has to cross between parts.
Inputs may be any that keep to these rules, and one draw needn't show every extreme that they name: `block_count`: at least one device holds 6 live block pairs in every draw.
All inputs are finite; a program needn't handle non-finite values.
Results may differ from a plain program's by a relative error of at most 0.00092.
Values may be sent and summed in bfloat16 or wider, within the bound.
No kernel may reach another device: no remote copies, remote signals or barrier semaphores. Data moves between devices by JAX's collectives and lax.ppermute only.
A program may use at most 64 MiB of HBM per device.

v0:
```python
import functools

import jax
import jax.numpy as jnp
from jax import lax
from jax.experimental import pallas as pl
from jax.experimental.pallas import tpu as pltpu
from jax.sharding import PartitionSpec as P

LANES = 128
TAIL = 16
TOP = 32700.0
LEAST = 2.0**-110


def code_scale(exponent, mantissa):
    return (mantissa * (1.0 / 16384.0)) * jnp.exp2(exponent)


def write_codes(blocks, msg_ref):
    rows, width = blocks[0]().shape
    panels = width // LANES
    top = None
    for load in blocks:
        high = jnp.max(jnp.abs(load()), axis=0, keepdims=True)
        for c in range(panels):
            part = high[:, c * LANES : (c + 1) * LANES]
            top = part if top is None else jnp.maximum(top, part)
    top = jnp.maximum(top, LEAST)
    exponent = jnp.ceil(jnp.log2(top))
    mantissa = jnp.ceil(top * jnp.exp2(-exponent) * 16384.0) + 1.0
    factor = TOP / code_scale(exponent, mantissa)
    for k, load in enumerate(blocks):
        for c in range(panels):
            part = load()[:, c * LANES : (c + 1) * LANES] * factor
            at = (k * panels + c) * rows
            msg_ref[at : at + rows, :] = jnp.round(part).astype(jnp.int32).astype(jnp.int16)
    line = lax.broadcasted_iota(jnp.int32, (TAIL, LANES), 0)
    tail = jnp.where(line == 0, exponent.astype(jnp.int32), mantissa.astype(jnp.int32))
    msg_ref[len(blocks) * panels * rows :, :] = tail.astype(jnp.int16)


def read_step(msg_ref):
    at = msg_ref.shape[0] - TAIL
    tail = msg_ref[at:, :].astype(jnp.int32).astype(jnp.float32)
    return code_scale(tail[0:1], tail[1:2]) * (1.0 / TOP)


def read_block(msg_ref, k, rows, panels, step):
    parts = []
    for c in range(panels):
        at = (k * panels + c) * rows
        parts.append(msg_ref[at : at + rows, :].astype(jnp.int32).astype(jnp.float32) * step)
    return jnp.concatenate(parts, axis=1)


def message_shape(count, rows, width):
    return jax.ShapeDtypeStruct((count * rows * (width // LANES) + TAIL, LANES), jnp.int16)


def block_offsets(groups, core):
    offsets = [0]
    for group in groups:
        offsets = [a ^ b for a in offsets for b in [0, *stage_offsets(group, core)]]
    return offsets


def stage_offsets(group, core):
    if len(group) == 1:
        return list(group)
    one, two = group if core == 0 else group[::-1]
    return [one | two, one, two]


def gram_kernel(plan, experts_in, count, teacher, student, gate, up, *rest):
    if plan is None:
        acc, x, w, hid, order, experts, x_sem, w_sem, s_sem = rest
    else:
        own, msg, x, w, hid, order, experts, acc, x_sem, w_sem, s_sem = rest
    slots, both, _ = x.shape
    block = both // 2
    expert_total, panels, _, pair_width = w.shape
    lanes = pair_width // 2
    width = panels * lanes

    def w_copies(e, c):
        cols = pl.ds(c * lanes, lanes)
        return [
            pltpu.make_async_copy(gate.at[e, :, cols], w.at[e, c, :, pl.ds(0, lanes)], w_sem.at[e, c, 0]),
            pltpu.make_async_copy(up.at[e, :, cols], w.at[e, c, :, pl.ds(lanes, lanes)], w_sem.at[e, c, 1]),
        ]

    scalars = [
        pltpu.make_async_copy(experts_in, experts, s_sem.at[0]),
    ]
    for copy in scalars:
        copy.start()
    for c in range(panels):
        for copy in w_copies(0, c):
            copy.start()
    for copy in scalars:
        copy.wait()
    live = count[0]

    keys = [jnp.where(s < live, experts[s], experts[s] + expert_total) for s in range(slots)]
    for s in range(slots):
        place = jnp.int32(0)
        for t in range(slots):
            if t != s:
                ahead = keys[t] <= keys[s] if t < s else keys[t] < keys[s]
                place = place + ahead.astype(jnp.int32)
        order[place] = s

    def expert_at(i):
        return experts[order[i]]

    def fresh(i):
        new = expert_at(i) != (expert_at(i - 1) if i else 0)
        return (i < live) & new

    def x_copies(i):
        rows = pl.ds(order[i] * block, block)
        return [
            pltpu.make_async_copy(student.at[rows], x.at[i, pl.ds(0, block)], x_sem.at[i, 0]),
            pltpu.make_async_copy(teacher.at[rows], x.at[i, pl.ds(block, block)], x_sem.at[i, 1]),
        ]

    def start_w(i):
        @pl.when(fresh(i))
        def _():
            for c in range(panels):
                for copy in w_copies(expert_at(i), c):
                    copy.start()

    def start_x(i):
        @pl.when(i < live)
        def _():
            for copy in x_copies(i):
                copy.start()

    def wait_w(i):
        @pl.when(fresh(i))
        def _():
            for c in range(panels):
                for copy in w_copies(expert_at(i), c):
                    copy.wait()

    def wait_x(i):
        @pl.when(i < live)
        def _():
            for copy in x_copies(i):
                copy.wait()

    start_x(0)
    start_w(0)
    acc[...] = jnp.zeros_like(acc)

    def hide(i):
        expert = expert_at(i)
        rows = pl.ds(i * block, block)
        for c in range(panels):
            out = jnp.dot(x[i], w[expert, c], preferred_element_type=jnp.float32)
            gate_out = out[:, :lanes]
            part = (gate_out / (1.0 + jnp.exp(-gate_out)) * out[:, lanes:]).astype(jnp.bfloat16)
            hid[rows, c * lanes : (c + 1) * lanes] = part[:block]
            hid[rows, width + c * lanes : width + (c + 1) * lanes] = part[block:]

    def add_product(expert, left, right):
        gram = lax.dot_general(left, right, (((0,), (0,)), ((), ())), preferred_element_type=jnp.float32)
        if plan is None:
            at = pl.ds(expert * width, width)
            acc[at] = acc[at] + gram
        else:
            per = width // acc.shape[1]
            at = pl.ds(expert * per, per)
            acc[at] = acc[at] + gram.reshape(per, *acc.shape[1:])

    def add_gram(i):
        rows = pl.ds(pl.multiple_of(i * block, block), block)
        add_product(expert_at(i), hid[rows, :width], hid[rows])

    for copy in w_copies(0, 0):
        copy.wait()
    for i in range(1, slots):
        start_w(i)
        start_x(i)
    wait_x(0)
    for c in range(1, panels):
        for copy in w_copies(0, c):
            copy.wait()
    wait_w(0)
    hide(0)

    @pl.when(live == slots)
    def _():
        for first, end in [(1, min(2, slots)), (2, slots)]:
            for i in range(first, end):
                wait_w(i)
            for i in range(first, end):
                for copy in x_copies(i):
                    copy.wait()
            for i in range(first, end):
                hide(i)
        for i in range(0, slots - 1, 2):
            same = expert_at(i) == expert_at(i + 1)
            two_rows = pl.ds(i * block, 2 * block)
            one_row = pl.ds((i + 1) * block, block)
            other = hid[one_row, :width]
            left = jnp.concatenate(
                [hid[pl.ds(i * block, block), :width], jnp.where(same, other, jnp.zeros_like(other))]
            )
            add_product(expert_at(i), left, hid[two_rows])
        for i in range(0, slots - 1, 2):

            @pl.when(expert_at(i) != expert_at(i + 1))
            def _():
                add_gram(i + 1)

        if slots % 2:
            add_gram(slots - 1)

    @pl.when(live < slots)
    def _():
        for i in range(1, slots - 1):

            @pl.when(i < live)
            def _():
                wait_w(i)
                for copy in x_copies(i):
                    copy.wait()
                hide(i)
                add_gram(i - 1)

        add_gram(live - 1)

    if plan is not None:
        me = lax.axis_index("dp")
        core = lax.rem(me, 2)
        chip = me // 2
        tables = [block_offsets(plan, c) for c in (0, 1)]
        loads = []
        for k in range(len(tables[0])):
            mine = jnp.where(core == 0, tables[0][k], tables[1][k])
            theirs = jnp.where(core == 0, tables[1][k], tables[0][k])
            own[k] = acc[2 * (chip ^ mine) + core]
            there = 2 * (chip ^ theirs) + (1 - core)
            loads.append(lambda there=there: acc[there])
        write_codes(loads, msg)


def grams(teacher, student, experts, count, gate, up, ranks, plan):
    slots = experts.shape[0]
    block = teacher.shape[0] // slots
    depth = teacher.shape[1]
    expert_total, _, width = gate.shape
    two = 2 * width
    rows = expert_total * width // ranks
    panels = width // LANES
    scratch = [
        pltpu.VMEM((slots, 2 * block, depth), jnp.bfloat16),
        pltpu.VMEM((expert_total, panels, depth, 2 * LANES), jnp.bfloat16),
        pltpu.VMEM((slots * block, two), jnp.bfloat16),
        pltpu.SMEM((slots,), jnp.int32),
        pltpu.SMEM((slots,), jnp.int32),
    ]
    sems = [
        pltpu.SemaphoreType.DMA((slots, 2)),
        pltpu.SemaphoreType.DMA((expert_total, panels, 2)),
        pltpu.SemaphoreType.DMA((1,)),
    ]
    if plan is None:
        out_shape = jax.ShapeDtypeStruct((expert_total * width, two), jnp.float32)
    else:
        scratch.append(pltpu.VMEM((ranks, rows, two), jnp.float32))
        out_shape = (
            jax.ShapeDtypeStruct((ranks // 2, rows, two), jnp.float32),
            message_shape(ranks // 2, rows, two),
        )
    hbm = pl.BlockSpec(memory_space=pl.ANY)
    return pl.pallas_call(
        functools.partial(gram_kernel, plan),
        out_shape=out_shape,
        in_specs=[hbm, pl.BlockSpec(memory_space=pltpu.SMEM), hbm, hbm, hbm, hbm],
        scratch_shapes=scratch + sems,
        compiler_params=pltpu.CompilerParams(vmem_limit_bytes=51 << 20),
        name="grams",
    )(pltpu.with_memory_space_constraint(experts, pltpu.HBM), count, *[pltpu.with_memory_space_constraint(a, pltpu.HBM) for a in (teacher, student, gate, up)])


def join_kernel(scaling, radix, parts, own, *rest):
    count, rows, width = own.shape
    panels = width // LANES
    msgs = rest[:parts]
    steps = [read_step(msg) for msg in msgs]

    def total(k):
        return own[k] + sum(
            read_block(msg, k, rows, panels, step) for msg, step in zip(msgs, steps)
        )

    if radix == 1:
        rest[parts][...] = total(0) * scaling
        return
    keep, *sends, held = rest[parts:]
    per = count // radix
    for k in range(per, count):
        held[k - per] = total(k)
    for d, send in enumerate(sends):
        write_codes([lambda k=k: held[k] for k in range(d * per, (d + 1) * per)], send)
    for k in range(per):
        keep[k] = total(k)


def join(own, msgs, radix, scaling):
    count, rows, width = own.shape
    if radix == 1:
        out_shape = jax.ShapeDtypeStruct((rows, width), jnp.float32)
        scratch = []
    else:
        per = count // radix
        out_shape = (
            jax.ShapeDtypeStruct((per, rows, width), jnp.float32),
            *[message_shape(per, rows, width)] * (radix - 1),
        )
        scratch = [pltpu.VMEM((count - per, rows, width), jnp.float32)]
    return pl.pallas_call(
        functools.partial(join_kernel, scaling, radix, len(msgs)),
        out_shape=out_shape,
        scratch_shapes=scratch,
        compiler_params=pltpu.CompilerParams(vmem_limit_bytes=32 << 20),
        name=f"join{count}",
    )(own, *msgs)


def local(teacher, student, experts, count, gate, up):
    ranks = lax.axis_size("dp")
    block = teacher.shape[0] // experts.shape[0]
    scaling = 1.0 / (block * ranks)
    total_rows = gate.shape[0] * gate.shape[2]
    rows = total_rows // ranks
    bits = ranks.bit_length() - 1
    coded = ranks >= 4 and ranks == 1 << bits and rows % 16 == 0 and gate.shape[2] % rows == 0
    if not coded:
        acc = grams(teacher, student, experts, count, gate, up, ranks, None)
        return lax.psum_scatter(acc, "dp", scatter_dimension=0, tiled=True) * scaling
    chip_bits = [1 << i for i in range(bits - 1)]
    groups = [tuple(chip_bits[i : i + 2]) for i in range(0, len(chip_bits), 2)]
    own, msg = grams(teacher, student, experts, count, gate, up, ranks, groups)
    msgs = [lax.ppermute(msg, "dp", [(p, p ^ 1) for p in range(ranks)])]
    for group in groups:
        own, *msgs = join(own, msgs, 1 << len(group), scaling)
        reach = [stage_offsets(group, core) for core in (0, 1)]
        msgs = [
            lax.ppermute(msg, "dp", [(p, p ^ (2 * reach[p % 2][i])) for p in range(ranks)])
            for i, msg in enumerate(msgs)
        ]
    return join(own, msgs, 1, scaling)


def solution(mesh):
    return jax.shard_map(
        local,
        mesh=mesh,
        in_specs=(
            P(("groups", "dp"), None),
            P(("groups", "dp"), None),
            P(("groups", "dp")),
            P(("groups", "dp")),
            P("groups", None, None),
            P("groups", None, None),
        ),
        out_specs=P(("groups", "dp"), None),
        check_vma=False,
    )
```

profile of v0, /device:TPU:0, one launch (start us, length us, event | category | flops | bytes accessed | tf_op | source)
XLA Modules:
  0.0 32.1 jit_solution(14567271441543987522)
XLA Ops:
  0.7 9.6 %grams.1 = (f32[8,48,768]{2,1,0:T(8,128)S(1)}, s16[2320,128]{1,0:T(8,128)(2,1)S(1)}) custom-call(s32[6]{0:T(128)} %experts_in.1, s32[1]{0:T(128)S(6)} %copy.7.count, bf16[768,2048]{1,0:T(8,128)(2,1)} %teacher.1, bf16[768,2048]{1,0:T(8,128)(2,1)} %student.1, bf16[2,2048,384]{2,1,0:T(8,128)(2,1)} %gate.1, bf16[2,2048,384]{2,1,0:T(8,128)(2,1)} %up.1), custom_call_target="tpu_custom_call" | custom-call | tf_op jit(solution)/shard_map/grams/pallas_call | solution.py:280
  10.3 0.1 collective-permute-start
  10.3 2.0 %collective-permute-done.rest_0_ = s16[2320,128]{1,0:T(8,128)(2,1)S(1)} collective-permute-done((s16[2320,128]{1,0:T(8,128)(2,1)S(1)}, s16[2320,128]{1,0:T(8,128)(2,1)S(1)}, u32[]{:S(2)}, u32[]{:S(2)}) %collective-permute-start) | collective-permute-done | bytes 593952 | tf_op jit(solution)/shard_map/ppermute | solution.py:349
  12.3 0.3 join8.1
  12.6 4.2 %collective-permute-start.1 = (s16[592,128]{1,0:T(8,128)(2,1)S(1)}, s16[592,128]{1,0:T(8,128)(2,1)S(1)}, u32[]{:S(2)}, u32[]{:S(2)}) collective-permute-start(s16[592,128]{1,0:T(8,128)(2,1)S(1)} %get-tuple-element.16), channel_id=1, source_target_pairs={{0,6},{1,7},{2,4},{3,5},{4,2},{5,3},{6,0},{7,1},{8,14},{9,15},{10,... | collective-permute-start | bytes 454664 | tf_op jit(solution)/shard_map/ppermute | solution.py:354
  16.8 0.0 collective-permute-start.2
  16.8 0.6 %collective-permute-start.3 = (s16[592,128]{1,0:T(8,128)(2,1)S(1)}, s16[592,128]{1,0:T(8,128)(2,1)S(1)}, u32[]{:S(2)}, u32[]{:S(2)}) collective-permute-start(s16[592,128]{1,0:T(8,128)(2,1)S(1)} %get-tuple-element.18), channel_id=1, source_target_pairs={{0,4},{1,3},{2,6},{3,1},{4,0},{5,7},{6,2},{7,5},{8,12},{9,11},{10,... | collective-permute-start | bytes 454664 | tf_op jit(solution)/shard_map/ppermute | solution.py:354
  17.5 4.1 %collective-permute-done.1.rest_0_ = s16[592,128]{1,0:T(8,128)(2,1)S(1)} collective-permute-done((s16[592,128]{1,0:T(8,128)(2,1)S(1)}, s16[592,128]{1,0:T(8,128)(2,1)S(1)}, u32[]{:S(2)}, u32[]{:S(2)}) %collective-permute-start.1) | collective-permute-done | bytes 151584 | tf_op jit(solution)/shard_map/ppermute | solution.py:354
  21.6 2.8 %collective-permute-done.2.rest_1_ = s16[592,128]{1,0:T(8,128)(2,1)S(1)} collective-permute-done((s16[592,128]{1,0:T(8,128)(2,1)S(1)}, s16[592,128]{1,0:T(8,128)(2,1)S(1)}, u32[]{:S(2)}, u32[]{:S(2)}) %collective-permute-start.2) | collective-permute-done | bytes 151584 | tf_op jit(solution)/shard_map/ppermute | solution.py:354
  24.3 0.0 collective-permute-done.3.rest_2_
  24.3 0.2 join2.1
  24.5 2.2 %collective-permute-start.4 = (s16[304,128]{1,0:T(8,128)(2,1)S(1)}, s16[304,128]{1,0:T(8,128)(2,1)S(1)}, u32[]{:S(2)}, u32[]{:S(2)}) collective-permute-start(s16[304,128]{1,0:T(8,128)(2,1)S(1)} %get-tuple-element.20), channel_id=1, source_target_pairs={{0,8},{1,9},{2,10},{3,11},{4,12},{5,13},{6,14},{7,15},{8,0},{9,1},... | collective-permute-start | bytes 233480 | tf_op jit(solution)/shard_map/ppermute | solution.py:354
  26.7 4.7 %collective-permute-done.4.rest_0_ = s16[304,128]{1,0:T(8,128)(2,1)S(1)} collective-permute-done((s16[304,128]{1,0:T(8,128)(2,1)S(1)}, s16[304,128]{1,0:T(8,128)(2,1)S(1)}, u32[]{:S(2)}, u32[]{:S(2)}) %collective-permute-start.4) | collective-permute-done | bytes 77856 | tf_op jit(solution)/shard_map/ppermute | solution.py:354
  31.4 0.7 %join1.1 = f32[48,768]{1,0:T(8,128)} custom-call(f32[1,48,768]{2,1,0:T(8,128)S(1)} %get-tuple-element.19.own, s16[304,128]{1,0:T(8,128)(2,1)S(1)} %collective-permute-done.4.rest_0_), custom_call_target="tpu_custom_call" | custom-call | tf_op jit(solution)/shard_map/join1/pallas_call | solution.py:326
Async XLA Ops:
  10.3 2.1 %collective-permute-start = (s16[2320,128]{1,0:T(8,128)(2,1)S(1)}, s16[2320,128]{1,0:T(8,128)(2,1)S(1)}, u32[]{:S(2)}, u32[]{:S(2)}) collective-permute-start(s16[2320,128]{1,0:T(8,128)(2,1)S(1)} %get-tuple-element.14), channel_id=1, source_target_pairs={{0,1},{1,0},{2,3},{3,2},{4,5},{5,4},{6,7},{7,6},{8,9},{9,8},{10,11... | collective-permute-start | bytes 1781768 | tf_op jit(solution)/shard_map/ppermute | solution.py:349
  12.6 8.9 %collective-permute-start.1 = (s16[592,128]{1,0:T(8,128)(2,1)S(1)}, s16[592,128]{1,0:T(8,128)(2,1)S(1)}, u32[]{:S(2)}, u32[]{:S(2)}) collective-permute-start(s16[592,128]{1,0:T(8,128)(2,1)S(1)} %get-tuple-element.16), channel_id=1, source_target_pairs={{0,6},{1,7},{2,4},{3,5},{4,2},{5,3},{6,0},{7,1},{8,14},{9,15},{10,... | collective-permute-start | bytes 454664 | tf_op jit(solution)/shard_map/ppermute | solution.py:354
  16.8 7.5 %collective-permute-start.2 = (s16[592,128]{1,0:T(8,128)(2,1)S(1)}, s16[592,128]{1,0:T(8,128)(2,1)S(1)}, u32[]{:S(2)}, u32[]{:S(2)}) collective-permute-start(s16[592,128]{1,0:T(8,128)(2,1)S(1)} %get-tuple-element.17), channel_id=1, source_target_pairs={{0,2},{1,5},{2,0},{3,7},{4,6},{5,1},{6,4},{7,3},{8,10},{9,13},{10,... | collective-permute-start | bytes 454664 | tf_op jit(solution)/shard_map/ppermute | solution.py:354
  16.8 7.5 %collective-permute-start.3 = (s16[592,128]{1,0:T(8,128)(2,1)S(1)}, s16[592,128]{1,0:T(8,128)(2,1)S(1)}, u32[]{:S(2)}, u32[]{:S(2)}) collective-permute-start(s16[592,128]{1,0:T(8,128)(2,1)S(1)} %get-tuple-element.18), channel_id=1, source_target_pairs={{0,4},{1,3},{2,6},{3,1},{4,0},{5,7},{6,2},{7,5},{8,12},{9,11},{10,... | collective-permute-start | bytes 454664 | tf_op jit(solution)/shard_map/ppermute | solution.py:354
  24.5 6.9 %collective-permute-start.4 = (s16[304,128]{1,0:T(8,128)(2,1)S(1)}, s16[304,128]{1,0:T(8,128)(2,1)S(1)}, u32[]{:S(2)}, u32[]{:S(2)}) collective-permute-start(s16[304,128]{1,0:T(8,128)(2,1)S(1)} %get-tuple-element.20), channel_id=1, source_target_pairs={{0,8},{1,9},{2,10},{3,11},{4,12},{5,13},{6,14},{7,15},{8,0},{9,1},... | collective-permute-start | bytes 233480 | tf_op jit(solution)/shard_map/ppermute | solution.py:354
where the time goes:
time: 32.2 us; the launch traced here: 32.1 us
  waiting for transfers between devices  13.5 us (42%)
  Pallas kernels  10.8 us (34%)
  starting transfers between devices  7.11 us (22%)
  between operations  0.68 us (2%)
    ppermute x4, waiting for transfers between devices, local(): lax.ppermute(msg, 'dp', [(p, p ^ 2 * reach[p % 2][i]) for p in range(rank...  11.5 us
    pallas_call x1, Pallas kernels, grams(): pl.pallas_call(functools.partial(gram_kernel, plan), out_shape=out_shape,...  9.6 us
    ppermute x4, starting transfers between devices, local(): lax.ppermute(msg, 'dp', [(p, p ^ 2 * reach[p % 2][i]) for p in range(rank...  7.04 us
    ppermute x1, waiting for transfers between devices, local(): msgs = [lax.ppermute(msg, 'dp', [(p, p ^ 1) for p in range(ranks)])]  2 us
    pallas_call x3, Pallas kernels, join(): pl.pallas_call(functools.partial(join_kernel, scaling, radix, len(msgs)),...  1.17 us
  transfers between devices with their start and end apart: 5, of which 4 were waited for; matrix products, arithmetic and copies ran while one was open for 0% of the time, Pallas kernels for 0%

commit v1 on v0

--- a/solution.py
+++ b/solution.py
@@ -58,9 +58,9 @@
     return jax.ShapeDtypeStruct((count * rows * (width // LANES) + TAIL, LANES), jnp.int16)
 
 
-def block_offsets(groups, core):
+def block_offsets(plan, core):
     offsets = [0]
-    for group in groups:
+    for group in plan[core]:
         offsets = [a ^ b for a in offsets for b in [0, *stage_offsets(group, core)]]
     return offsets
 
@@ -344,12 +344,13 @@
         acc = grams(teacher, student, experts, count, gate, up, ranks, None)
         return lax.psum_scatter(acc, "dp", scatter_dimension=0, tiled=True) * scaling
     chip_bits = [1 << i for i in range(bits - 1)]
-    groups = [tuple(chip_bits[i : i + 2]) for i in range(0, len(chip_bits), 2)]
-    own, msg = grams(teacher, student, experts, count, gate, up, ranks, groups)
+    orders = [chip_bits, chip_bits[:1] + chip_bits[2:3] + chip_bits[1:2] + chip_bits[3:]]
+    plan = [[tuple(bits[i : i + 2]) for i in range(0, len(bits), 2)] for bits in orders]
+    own, msg = grams(teacher, student, experts, count, gate, up, ranks, plan)
     msgs = [lax.ppermute(msg, "dp", [(p, p ^ 1) for p in range(ranks)])]
-    for group in groups:
-        own, *msgs = join(own, msgs, 1 << len(group), scaling)
-        reach = [stage_offsets(group, core) for core in (0, 1)]
+    for pair in zip(*plan):
+        own, *msgs = join(own, msgs, 1 << len(pair[0]), scaling)
+        reach = [stage_offsets(group, core) for core, group in enumerate(pair)]
         msgs = [
             lax.ppermute(msg, "dp", [(p, p ^ (2 * reach[p % 2][i])) for p in range(ranks)])
             for i, msg in enumerate(msgs)

time: 32.2 us -> 30.7 us (0.953)
  the two profiles are of different devices: /device:TPU:0 before, /device:TPU:4 now
where the time goes in v1:
time: 30.7 us; the launch traced here: 30.2 us
  waiting for transfers between devices  12.2 us (40%)
  starting transfers between devices  10.8 us (35%)
  Pallas kernels  6.63 us (22%)
  between operations  0.68 us (2%)
    ppermute x4, starting transfers between devices, local(): lax.ppermute(msg, 'dp', [(p, p ^ 2 * reach[p % 2][i]) for p in range(rank...  10.7 us
    ppermute x4, waiting for transfers between devices, local(): lax.ppermute(msg, 'dp', [(p, p ^ 2 * reach[p % 2][i]) for p in range(rank...  10.2 us
    pallas_call x1, Pallas kernels, grams(): pl.pallas_call(functools.partial(gram_kernel, plan), out_shape=out_shape,...  5.46 us
    ppermute x1, waiting for transfers between devices, local(): msgs = [lax.ppermute(msg, 'dp', [(p, p ^ 1) for p in range(ranks)])]  2 us
    pallas_call x3, Pallas kernels, join(): pl.pallas_call(functools.partial(join_kernel, scaling, radix, len(msgs)),...  1.17 us
  transfers between devices with their start and end apart: 5, of which 5 were waited for; matrix products, arithmetic and copies ran while one was open for 0% of the time, Pallas kernels for 0%

profile of v1, /device:TPU:4, one launch (start us, length us, event | category | flops | bytes accessed | tf_op | source)
XLA Modules:
  0.0 30.2 jit_solution(15478333142028322658)
XLA Ops:
  0.7 5.5 %grams.1 = (f32[8,48,768]{2,1,0:T(8,128)S(1)}, s16[2320,128]{1,0:T(8,128)(2,1)S(1)}) custom-call(s32[6]{0:T(128)} %experts_in.1, s32[1]{0:T(128)S(6)} %copy.7.count, bf16[768,2048]{1,0:T(8,128)(2,1)} %teacher.1, bf16[768,2048]{1,0:T(8,128)(2,1)} %student.1, bf16[2,2048,384]{2,1,0:T(8,128)(2,1)} %gate.1, bf16[2,2048,384]{2,1,0:T(8,128)(2,1)} %up.1), custom_call_target="tpu_custom_call" | custom-call | tf_op jit(solution)/shard_map/grams/pallas_call | solution.py:280
  6.1 0.1 collective-permute-start
  6.2 2.0 %collective-permute-done.rest_0_ = s16[2320,128]{1,0:T(8,128)(2,1)S(1)} collective-permute-done((s16[2320,128]{1,0:T(8,128)(2,1)S(1)}, s16[2320,128]{1,0:T(8,128)(2,1)S(1)}, u32[]{:S(2)}, u32[]{:S(2)}) %collective-permute-start) | collective-permute-done | bytes 593952 | tf_op jit(solution)/shard_map/ppermute | solution.py:350
  8.2 0.3 %join8.1 = (f32[2,48,768]{2,1,0:T(8,128)S(1)}, s16[592,128]{1,0:T(8,128)(2,1)S(1)}, s16[592,128]{1,0:T(8,128)(2,1)S(1)}, s16[592,128]{1,0:T(8,128)(2,1)S(1)}) custom-call(f32[8,48,768]{2,1,0:T(8,128)S(1)} %get-tuple-element.13.own, s16[2320,128]{1,0:T(8,128)(2,1)S(1)} %collective-permute-done.rest_0_), custom_call_target="tpu_custom_call" | custom-call | tf_op jit(solution)/shard_map/join8/pallas_call | solution.py:326
  8.5 1.3 %collective-permute-start.1 = (s16[592,128]{1,0:T(8,128)(2,1)S(1)}, s16[592,128]{1,0:T(8,128)(2,1)S(1)}, u32[]{:S(2)}, u32[]{:S(2)}) collective-permute-start(s16[592,128]{1,0:T(8,128)(2,1)S(1)} %get-tuple-element.16), channel_id=1, source_target_pairs={{0,6},{1,11},{2,4},{3,9},{4,2},{5,15},{6,0},{7,13},{8,14},{9,3},{1... | collective-permute-start | bytes 454664 | tf_op jit(solution)/shard_map/ppermute | solution.py:355
  9.8 2.7 %collective-permute-start.2 = (s16[592,128]{1,0:T(8,128)(2,1)S(1)}, s16[592,128]{1,0:T(8,128)(2,1)S(1)}, u32[]{:S(2)}, u32[]{:S(2)}) collective-permute-start(s16[592,128]{1,0:T(8,128)(2,1)S(1)} %get-tuple-element.17), channel_id=1, source_target_pairs={{0,2},{1,9},{2,0},{3,11},{4,6},{5,13},{6,4},{7,15},{8,10},{9,1},{1... | collective-permute-start | bytes 454664 | tf_op jit(solution)/shard_map/ppermute | solution.py:355
  12.5 0.0 collective-permute-start.3
  12.5 3.8 %collective-permute-done.1.rest_0_ = s16[592,128]{1,0:T(8,128)(2,1)S(1)} collective-permute-done((s16[592,128]{1,0:T(8,128)(2,1)S(1)}, s16[592,128]{1,0:T(8,128)(2,1)S(1)}, u32[]{:S(2)}, u32[]{:S(2)}) %collective-permute-start.1) | collective-permute-done | bytes 151584 | tf_op jit(solution)/shard_map/ppermute | solution.py:355
  16.4 1.5 %collective-permute-done.2.rest_1_ = s16[592,128]{1,0:T(8,128)(2,1)S(1)} collective-permute-done((s16[592,128]{1,0:T(8,128)(2,1)S(1)}, s16[592,128]{1,0:T(8,128)(2,1)S(1)}, u32[]{:S(2)}, u32[]{:S(2)}) %collective-permute-start.2) | collective-permute-done | bytes 151584 | tf_op jit(solution)/shard_map/ppermute | solution.py:355
  17.9 1.6 %collective-permute-done.3.rest_2_ = s16[592,128]{1,0:T(8,128)(2,1)S(1)} collective-permute-done((s16[592,128]{1,0:T(8,128)(2,1)S(1)}, s16[592,128]{1,0:T(8,128)(2,1)S(1)}, u32[]{:S(2)}, u32[]{:S(2)}) %collective-permute-start.3) | collective-permute-done | bytes 151584 | tf_op jit(solution)/shard_map/ppermute | solution.py:355
  19.5 0.2 join2.1
  19.7 6.7 %collective-permute-start.4 = (s16[304,128]{1,0:T(8,128)(2,1)S(1)}, s16[304,128]{1,0:T(8,128)(2,1)S(1)}, u32[]{:S(2)}, u32[]{:S(2)}) collective-permute-start(s16[304,128]{1,0:T(8,128)(2,1)S(1)} %get-tuple-element.20), channel_id=1, source_target_pairs={{0,8},{1,5},{2,10},{3,7},{4,12},{5,1},{6,14},{7,3},{8,0},{9,13},{1... | collective-permute-start | bytes 233480 | tf_op jit(solution)/shard_map/ppermute | solution.py:355
  26.3 3.2 %collective-permute-done.4.rest_0_ = s16[304,128]{1,0:T(8,128)(2,1)S(1)} collective-permute-done((s16[304,128]{1,0:T(8,128)(2,1)S(1)}, s16[304,128]{1,0:T(8,128)(2,1)S(1)}, u32[]{:S(2)}, u32[]{:S(2)}) %collective-permute-start.4) | collective-permute-done | bytes 77856 | tf_op jit(solution)/shard_map/ppermute | solution.py:355
  29.6 0.7 %join1.1 = f32[48,768]{1,0:T(8,128)} custom-call(f32[1,48,768]{2,1,0:T(8,128)S(1)} %get-tuple-element.19.own, s16[304,128]{1,0:T(8,128)(2,1)S(1)} %collective-permute-done.4.rest_0_), custom_call_target="tpu_custom_call" | custom-call | tf_op jit(solution)/shard_map/join1/pallas_call | solution.py:326
Async XLA Ops:
  6.1 2.1 %collective-permute-start = (s16[2320,128]{1,0:T(8,128)(2,1)S(1)}, s16[2320,128]{1,0:T(8,128)(2,1)S(1)}, u32[]{:S(2)}, u32[]{:S(2)}) collective-permute-start(s16[2320,128]{1,0:T(8,128)(2,1)S(1)} %get-tuple-element.14), channel_id=1, source_target_pairs={{0,1},{1,0},{2,3},{3,2},{4,5},{5,4},{6,7},{7,6},{8,9},{9,8},{10,11... | collective-permute-start | bytes 1781768 | tf_op jit(solution)/shard_map/ppermute | solution.py:350
  8.5 7.9 %collective-permute-start.1 = (s16[592,128]{1,0:T(8,128)(2,1)S(1)}, s16[592,128]{1,0:T(8,128)(2,1)S(1)}, u32[]{:S(2)}, u32[]{:S(2)}) collective-permute-start(s16[592,128]{1,0:T(8,128)(2,1)S(1)} %get-tuple-element.16), channel_id=1, source_target_pairs={{0,6},{1,11},{2,4},{3,9},{4,2},{5,15},{6,0},{7,13},{8,14},{9,3},{1... | collective-permute-start | bytes 454664 | tf_op jit(solution)/shard_map/ppermute | solution.py:355
  9.8 8.1 %collective-permute-start.2 = (s16[592,128]{1,0:T(8,128)(2,1)S(1)}, s16[592,128]{1,0:T(8,128)(2,1)S(1)}, u32[]{:S(2)}, u32[]{:S(2)}) collective-permute-start(s16[592,128]{1,0:T(8,128)(2,1)S(1)} %get-tuple-element.17), channel_id=1, source_target_pairs={{0,2},{1,9},{2,0},{3,11},{4,6},{5,13},{6,4},{7,15},{8,10},{9,1},{1... | collective-permute-start | bytes 454664 | tf_op jit(solution)/shard_map/ppermute | solution.py:355
  12.5 6.9 %collective-permute-start.3 = (s16[592,128]{1,0:T(8,128)(2,1)S(1)}, s16[592,128]{1,0:T(8,128)(2,1)S(1)}, u32[]{:S(2)}, u32[]{:S(2)}) collective-permute-start(s16[592,128]{1,0:T(8,128)(2,1)S(1)} %get-tuple-element.18), channel_id=1, source_target_pairs={{0,4},{1,3},{2,6},{3,1},{4,0},{5,7},{6,2},{7,5},{8,12},{9,11},{10,... | collective-permute-start | bytes 454664 | tf_op jit(solution)/shard_map/ppermute | solution.py:355
  19.7 9.9 %collective-permute-start.4 = (s16[304,128]{1,0:T(8,128)(2,1)S(1)}, s16[304,128]{1,0:T(8,128)(2,1)S(1)}, u32[]{:S(2)}, u32[]{:S(2)}) collective-permute-start(s16[304,128]{1,0:T(8,128)(2,1)S(1)} %get-tuple-element.20), channel_id=1, source_target_pairs={{0,8},{1,5},{2,10},{3,7},{4,12},{5,1},{6,14},{7,3},{8,0},{9,13},{1... | collective-permute-start | bytes 233480 | tf_op jit(solution)/shard_map/ppermute | solution.py:355

commit v2 on v1

--- a/solution.py
+++ b/solution.py
@@ -68,8 +68,8 @@
 def stage_offsets(group, core):
     if len(group) == 1:
         return list(group)
-    one, two = group if core == 0 else group[::-1]
-    return [one | two, one, two]
+    one, two = group
+    return [one, one | two, two] if core == 0 else [two, one, one | two]
 
 
 def gram_kernel(plan, experts_in, count, teacher, student, gate, up, *rest):

time: 30.7 us -> 30 us (0.977)
  the two profiles are of different devices: /device:TPU:4 before, /device:TPU:0 now
where the time goes in v2:
time: 30 us; the launch traced here: 29.8 us
  starting transfers between devices  11.6 us (39%)
  waiting for transfers between devices  10.7 us (36%)
  Pallas kernels  6.77 us (23%)
  between operations  0.67 us (2%)
    ppermute x4, waiting for transfers between devices, local(): lax.ppermute(msg, 'dp', [(p, p ^ 2 * reach[p % 2][i]) for p in range(rank...  9.04 us
    ppermute x4, starting transfers between devices, local(): lax.ppermute(msg, 'dp', [(p, p ^ 2 * reach[p % 2][i]) for p in range(rank...  6.79 us
    pallas_call x1, Pallas kernels, grams(): pl.pallas_call(functools.partial(gram_kernel, plan), out_shape=out_shape,...  5.6 us
    ppermute x1, starting transfers between devices, local(): msgs = [lax.ppermute(msg, 'dp', [(p, p ^ 1) for p in range(ranks)])]  4.85 us
    ppermute x1, waiting for transfers between devices, local(): msgs = [lax.ppermute(msg, 'dp', [(p, p ^ 1) for p in range(ranks)])]  1.64 us
    pallas_call x3, Pallas kernels, join(): pl.pallas_call(functools.partial(join_kernel, scaling, radix, len(msgs)),...  1.17 us
  transfers between devices with their start and end apart: 5, of which 5 were waited for; matrix products, arithmetic and copies ran while one was open for 0% of the time, Pallas kernels for 0%

profile of v2, /device:TPU:0, one launch (start us, length us, event | category | flops | bytes accessed | tf_op | source)
XLA Modules:
  0.0 29.8 jit_solution(13075368043709571551)
XLA Ops:
  0.7 5.6 %grams.1 = (f32[8,48,768]{2,1,0:T(8,128)S(1)}, s16[2320,128]{1,0:T(8,128)(2,1)S(1)}) custom-call(s32[6]{0:T(128)} %experts_in.1, s32[1]{0:T(128)S(6)} %copy.7.count, bf16[768,2048]{1,0:T(8,128)(2,1)} %teacher.1, bf16[768,2048]{1,0:T(8,128)(2,1)} %student.1, bf16[2,2048,384]{2,1,0:T(8,128)(2,1)} %gate.1, bf16[2,2048,384]{2,1,0:T(8,128)(2,1)} %up.1), custom_call_target="tpu_custom_call" | custom-call | tf_op jit(solution)/shard_map/grams/pallas_call | solution.py:280
  6.3 4.8 %collective-permute-start = (s16[2320,128]{1,0:T(8,128)(2,1)S(1)}, s16[2320,128]{1,0:T(8,128)(2,1)S(1)}, u32[]{:S(2)}, u32[]{:S(2)}) collective-permute-start(s16[2320,128]{1,0:T(8,128)(2,1)S(1)} %get-tuple-element.14), channel_id=1, source_target_pairs={{0,1},{1,0},{2,3},{3,2},{4,5},{5,4},{6,7},{7,6},{8,9},{9,8},{10,11... | collective-permute-start | bytes 1781768 | tf_op jit(solution)/shard_map/ppermute | solution.py:350
  11.1 1.6 %collective-permute-done.rest_0_ = s16[2320,128]{1,0:T(8,128)(2,1)S(1)} collective-permute-done((s16[2320,128]{1,0:T(8,128)(2,1)S(1)}, s16[2320,128]{1,0:T(8,128)(2,1)S(1)}, u32[]{:S(2)}, u32[]{:S(2)}) %collective-permute-start) | collective-permute-done | bytes 593952 | tf_op jit(solution)/shard_map/ppermute | solution.py:350
  12.7 0.3 %join8.1 = (f32[2,48,768]{2,1,0:T(8,128)S(1)}, s16[592,128]{1,0:T(8,128)(2,1)S(1)}, s16[592,128]{1,0:T(8,128)(2,1)S(1)}, s16[592,128]{1,0:T(8,128)(2,1)S(1)}) custom-call(f32[8,48,768]{2,1,0:T(8,128)S(1)} %get-tuple-element.13.own, s16[2320,128]{1,0:T(8,128)(2,1)S(1)} %collective-permute-done.rest_0_), custom_call_target="tpu_custom_call" | custom-call | tf_op jit(solution)/shard_map/join8/pallas_call | solution.py:326
  13.1 2.6 %collective-permute-start.1 = (s16[592,128]{1,0:T(8,128)(2,1)S(1)}, s16[592,128]{1,0:T(8,128)(2,1)S(1)}, u32[]{:S(2)}, u32[]{:S(2)}) collective-permute-start(s16[592,128]{1,0:T(8,128)(2,1)S(1)} %get-tuple-element.16), channel_id=1, source_target_pairs={{0,2},{1,9},{2,0},{3,11},{4,6},{5,13},{6,4},{7,15},{8,10},{9,1},{1... | collective-permute-start | bytes 454664 | tf_op jit(solution)/shard_map/ppermute | solution.py:355
  15.7 1.3 %collective-permute-start.2 = (s16[592,128]{1,0:T(8,128)(2,1)S(1)}, s16[592,128]{1,0:T(8,128)(2,1)S(1)}, u32[]{:S(2)}, u32[]{:S(2)}) collective-permute-start(s16[592,128]{1,0:T(8,128)(2,1)S(1)} %get-tuple-element.17), channel_id=1, source_target_pairs={{0,6},{1,3},{2,4},{3,1},{4,2},{5,7},{6,0},{7,5},{8,14},{9,11},{10,... | collective-permute-start | bytes 454664 | tf_op jit(solution)/shard_map/ppermute | solution.py:355
  17.0 0.2 collective-permute-start.3
  17.2 4.1 %collective-permute-done.1.rest_0_ = s16[592,128]{1,0:T(8,128)(2,1)S(1)} collective-permute-done((s16[592,128]{1,0:T(8,128)(2,1)S(1)}, s16[592,128]{1,0:T(8,128)(2,1)S(1)}, u32[]{:S(2)}, u32[]{:S(2)}) %collective-permute-start.1) | collective-permute-done | bytes 151584 | tf_op jit(solution)/shard_map/ppermute | solution.py:355
  21.3 1.6 %collective-permute-done.2.rest_1_ = s16[592,128]{1,0:T(8,128)(2,1)S(1)} collective-permute-done((s16[592,128]{1,0:T(8,128)(2,1)S(1)}, s16[592,128]{1,0:T(8,128)(2,1)S(1)}, u32[]{:S(2)}, u32[]{:S(2)}) %collective-permute-start.2) | collective-permute-done | bytes 151584 | tf_op jit(solution)/shard_map/ppermute | solution.py:355
  22.9 0.6 %collective-permute-done.3.rest_2_ = s16[592,128]{1,0:T(8,128)(2,1)S(1)} collective-permute-done((s16[592,128]{1,0:T(8,128)(2,1)S(1)}, s16[592,128]{1,0:T(8,128)(2,1)S(1)}, u32[]{:S(2)}, u32[]{:S(2)}) %collective-permute-start.3) | collective-permute-done | bytes 151584 | tf_op jit(solution)/shard_map/ppermute | solution.py:355
  23.5 0.2 join2.1
  23.7 2.6 %collective-permute-start.4 = (s16[304,128]{1,0:T(8,128)(2,1)S(1)}, s16[304,128]{1,0:T(8,128)(2,1)S(1)}, u32[]{:S(2)}, u32[]{:S(2)}) collective-permute-start(s16[304,128]{1,0:T(8,128)(2,1)S(1)} %get-tuple-element.20), channel_id=1, source_target_pairs={{0,8},{1,5},{2,10},{3,7},{4,12},{5,1},{6,14},{7,3},{8,0},{9,13},{1... | collective-permute-start | bytes 233480 | tf_op jit(solution)/shard_map/ppermute | solution.py:355
  26.3 2.7 %collective-permute-done.4.rest_0_ = s16[304,128]{1,0:T(8,128)(2,1)S(1)} collective-permute-done((s16[304,128]{1,0:T(8,128)(2,1)S(1)}, s16[304,128]{1,0:T(8,128)(2,1)S(1)}, u32[]{:S(2)}, u32[]{:S(2)}) %collective-permute-start.4) | collective-permute-done | bytes 77856 | tf_op jit(solution)/shard_map/ppermute | solution.py:355
  29.1 0.7 %join1.1 = f32[48,768]{1,0:T(8,128)} custom-call(f32[1,48,768]{2,1,0:T(8,128)S(1)} %get-tuple-element.19.own, s16[304,128]{1,0:T(8,128)(2,1)S(1)} %collective-permute-done.4.rest_0_), custom_call_target="tpu_custom_call" | custom-call | tf_op jit(solution)/shard_map/join1/pallas_call | solution.py:326
Async XLA Ops:
  6.3 6.5 %collective-permute-start = (s16[2320,128]{1,0:T(8,128)(2,1)S(1)}, s16[2320,128]{1,0:T(8,128)(2,1)S(1)}, u32[]{:S(2)}, u32[]{:S(2)}) collective-permute-start(s16[2320,128]{1,0:T(8,128)(2,1)S(1)} %get-tuple-element.14), channel_id=1, source_target_pairs={{0,1},{1,0},{2,3},{3,2},{4,5},{5,4},{6,7},{7,6},{8,9},{9,8},{10,11... | collective-permute-start | bytes 1781768 | tf_op jit(solution)/shard_map/ppermute | solution.py:350
  13.1 8.2 %collective-permute-start.1 = (s16[592,128]{1,0:T(8,128)(2,1)S(1)}, s16[592,128]{1,0:T(8,128)(2,1)S(1)}, u32[]{:S(2)}, u32[]{:S(2)}) collective-permute-start(s16[592,128]{1,0:T(8,128)(2,1)S(1)} %get-tuple-element.16), channel_id=1, source_target_pairs={{0,2},{1,9},{2,0},{3,11},{4,6},{5,13},{6,4},{7,15},{8,10},{9,1},{1... | collective-permute-start | bytes 454664 | tf_op jit(solution)/shard_map/ppermute | solution.py:355
  15.7 7.3 %collective-permute-start.2 = (s16[592,128]{1,0:T(8,128)(2,1)S(1)}, s16[592,128]{1,0:T(8,128)(2,1)S(1)}, u32[]{:S(2)}, u32[]{:S(2)}) collective-permute-start(s16[592,128]{1,0:T(8,128)(2,1)S(1)} %get-tuple-element.17), channel_id=1, source_target_pairs={{0,6},{1,3},{2,4},{3,1},{4,2},{5,7},{6,0},{7,5},{8,14},{9,11},{10,... | collective-permute-start | bytes 454664 | tf_op jit(solution)/shard_map/ppermute | solution.py:355
  17.0 6.5 %collective-permute-start.3 = (s16[592,128]{1,0:T(8,128)(2,1)S(1)}, s16[592,128]{1,0:T(8,128)(2,1)S(1)}, u32[]{:S(2)}, u32[]{:S(2)}) collective-permute-start(s16[592,128]{1,0:T(8,128)(2,1)S(1)} %get-tuple-element.18), channel_id=1, source_target_pairs={{0,4},{1,11},{2,6},{3,9},{4,0},{5,15},{6,2},{7,13},{8,12},{9,3},{1... | collective-permute-start | bytes 454664 | tf_op jit(solution)/shard_map/ppermute | solution.py:355
  23.7 5.4 %collective-permute-start.4 = (s16[304,128]{1,0:T(8,128)(2,1)S(1)}, s16[304,128]{1,0:T(8,128)(2,1)S(1)}, u32[]{:S(2)}, u32[]{:S(2)}) collective-permute-start(s16[304,128]{1,0:T(8,128)(2,1)S(1)} %get-tuple-element.20), channel_id=1, source_target_pairs={{0,8},{1,5},{2,10},{3,7},{4,12},{5,1},{6,14},{7,3},{8,0},{9,13},{1... | collective-permute-start | bytes 233480 | tf_op jit(solution)/shard_map/ppermute | solution.py:355

commit v3 on v2

--- a/solution.py
+++ b/solution.py
@@ -72,11 +72,22 @@
     return [one, one | two, two] if core == 0 else [two, one, one | two]
 
 
+def block_places(plan):
+    me = lax.axis_index("dp")
+    core = lax.rem(me, 2)
+    chip = me // 2
+    mine, there = [], []
+    for zero, one in zip(block_offsets(plan, 0), block_offsets(plan, 1)):
+        mine.append(2 * (chip ^ jnp.where(core == 0, zero, one)) + core)
+        there.append(2 * (chip ^ jnp.where(core == 0, one, zero)) + (1 - core))
+    return mine, there
+
+
 def gram_kernel(plan, experts_in, count, teacher, student, gate, up, *rest):
     if plan is None:
         acc, x, w, hid, order, experts, x_sem, w_sem, s_sem = rest
     else:
-        own, msg, x, w, hid, order, experts, acc, x_sem, w_sem, s_sem = rest
+        acc, msg, x, w, hid, order, experts, x_sem, w_sem, s_sem = rest
     slots, both, _ = x.shape
     block = both // 2
     expert_total, panels, _, pair_width = w.shape
@@ -234,17 +245,8 @@
         add_gram(live - 1)
 
     if plan is not None:
-        me = lax.axis_index("dp")
-        core = lax.rem(me, 2)
-        chip = me // 2
-        tables = [block_offsets(plan, c) for c in (0, 1)]
-        loads = []
-        for k in range(len(tables[0])):
-            mine = jnp.where(core == 0, tables[0][k], tables[1][k])
-            theirs = jnp.where(core == 0, tables[1][k], tables[0][k])
-            own[k] = acc[2 * (chip ^ mine) + core]
-            there = 2 * (chip ^ theirs) + (1 - core)
-            loads.append(lambda there=there: acc[there])
+        _, there = block_places(plan)
+        loads = [lambda k=k: acc[k] for k in there]
         write_codes(loads, msg)
 
 
@@ -271,9 +273,8 @@
     if plan is None:
         out_shape = jax.ShapeDtypeStruct((expert_total * width, two), jnp.float32)
     else:
-        scratch.append(pltpu.VMEM((ranks, rows, two), jnp.float32))
         out_shape = (
-            jax.ShapeDtypeStruct((ranks // 2, rows, two), jnp.float32),
+            jax.ShapeDtypeStruct((ranks, rows, two), jnp.float32),
             message_shape(ranks // 2, rows, two),
         )
     hbm = pl.BlockSpec(memory_space=pl.ANY)
@@ -282,19 +283,23 @@
         out_shape=out_shape,
         in_specs=[hbm, pl.BlockSpec(memory_space=pltpu.SMEM), hbm, hbm, hbm, hbm],
         scratch_shapes=scratch + sems,
-        compiler_params=pltpu.CompilerParams(vmem_limit_bytes=51 << 20),
+        compiler_params=pltpu.CompilerParams(vmem_limit_bytes=49 << 20),
         name="grams",
     )(pltpu.with_memory_space_constraint(experts, pltpu.HBM), count, *[pltpu.with_memory_space_constraint(a, pltpu.HBM) for a in (teacher, student, gate, up)])
 
 
-def join_kernel(scaling, radix, parts, own, *rest):
+def join_kernel(scaling, radix, parts, plan, own, *rest):
     count, rows, width = own.shape
+    places = list(range(count))
+    if plan is not None:
+        places, _ = block_places(plan)
+        count = len(places)
     panels = width // LANES
     msgs = rest[:parts]
     steps = [read_step(msg) for msg in msgs]
 
     def total(k):
-        return own[k] + sum(
+        return own[places[k]] + sum(
             read_block(msg, k, rows, panels, step) for msg, step in zip(msgs, steps)
         )
 
@@ -311,8 +316,10 @@
         keep[k] = total(k)
 
 
-def join(own, msgs, radix, scaling):
+def join(own, msgs, radix, scaling, plan=None):
     count, rows, width = own.shape
+    if plan is not None:
+        count //= 2
     if radix == 1:
         out_shape = jax.ShapeDtypeStruct((rows, width), jnp.float32)
         scratch = []
@@ -324,7 +331,7 @@
         )
         scratch = [pltpu.VMEM((count - per, rows, width), jnp.float32)]
     return pl.pallas_call(
-        functools.partial(join_kernel, scaling, radix, len(msgs)),
+        functools.partial(join_kernel, scaling, radix, len(msgs), plan),
         out_shape=out_shape,
         scratch_shapes=scratch,
         compiler_params=pltpu.CompilerParams(vmem_limit_bytes=32 << 20),
@@ -348,8 +355,8 @@
     plan = [[tuple(bits[i : i + 2]) for i in range(0, len(bits), 2)] for bits in orders]
     own, msg = grams(teacher, student, experts, count, gate, up, ranks, plan)
     msgs = [lax.ppermute(msg, "dp", [(p, p ^ 1) for p in range(ranks)])]
-    for pair in zip(*plan):
-        own, *msgs = join(own, msgs, 1 << len(pair[0]), scaling)
+    for stage, pair in enumerate(zip(*plan)):
+        own, *msgs = join(own, msgs, 1 << len(pair[0]), scaling, None if stage else plan)
         reach = [stage_offsets(group, core) for core, group in enumerate(pair)]
         msgs = [
             lax.ppermute(msg, "dp", [(p, p ^ (2 * reach[p % 2][i])) for p in range(ranks)])

time: 30 us -> 30.9 us (1.030)
  waiting for transfers between devices: 10.7 us -> 11.8 us
    ppermute x1, starting transfers between devices: 4.85 us -> 0.1 us  [local(): msgs = [lax.ppermute(msg, 'dp', [(p, p ^ 1) for p in range(ranks)])]]
    ppermute x4, starting transfers between devices: 6.79 us -> 11.5 us  [local(): lax.ppermute(msg, 'dp', [(p, p ^ 2 * reach[p % 2][i]) for p in range(rank...]
    ppermute x4, waiting for transfers between devices: 9.04 us -> 9.83 us  [local(): lax.ppermute(msg, 'dp', [(p, p ^ 2 * reach[p % 2][i]) for p in range(rank...]
    ppermute x1, waiting for transfers between devices: 1.64 us -> 1.97 us  [local(): msgs = [lax.ppermute(msg, 'dp', [(p, p ^ 1) for p in range(ranks)])]]
  transfers between devices with their start and end apart: 5 -> 5, of which waited for: 5 -> 4; matrix products, arithmetic and copies ran while one was open for 0% -> 0% of each run, Pallas kernels for 0% -> 0%
where the time goes in v3:
time: 30.9 us; the launch traced here: 30.7 us
  waiting for transfers between devices  11.8 us (38%)
  starting transfers between devices  11.6 us (38%)
  Pallas kernels  6.72 us (22%)
  between operations  0.68 us (2%)
    ppermute x4, starting transfers between devices, local(): lax.ppermute(msg, 'dp', [(p, p ^ 2 * reach[p % 2][i]) for p in range(rank...  11.5 us
    ppermute x4, waiting for transfers between devices, local(): lax.ppermute(msg, 'dp', [(p, p ^ 2 * reach[p % 2][i]) for p in range(rank...  9.83 us
    pallas_call x1, Pallas kernels, grams(): pl.pallas_call(functools.partial(gram_kernel, plan), out_shape=out_shape,...  5.53 us
    ppermute x1, waiting for transfers between devices, local(): msgs = [lax.ppermute(msg, 'dp', [(p, p ^ 1) for p in range(ranks)])]  1.97 us
    pallas_call x3, Pallas kernels, join(): pl.pallas_call(functools.partial(join_kernel, scaling, radix, len(msgs),...  1.19 us
  transfers between devices with their start and end apart: 5, of which 4 were waited for; matrix products, arithmetic and copies ran while one was open for 0% of the time, Pallas kernels for 0%

profile of v3, /device:TPU:0, one launch (start us, length us, event | category | flops | bytes accessed | tf_op | source)
XLA Modules:
  0.0 30.7 jit_solution(17719622004779478913)
XLA Ops:
  0.7 5.5 %grams.1 = (f32[16,48,768]{2,1,0:T(8,128)S(1)}, s16[2320,128]{1,0:T(8,128)(2,1)S(1)}) custom-call(s32[6]{0:T(128)} %experts_in.1, s32[1]{0:T(128)S(6)} %copy.7.count, bf16[768,2048]{1,0:T(8,128)(2,1)} %teacher.1, bf16[768,2048]{1,0:T(8,128)(2,1)} %student.1, bf16[2,2048,384]{2,1,0:T(8,128)(2,1)} %gate.1, bf16[2,2048,384]{2,1,0:T(8,128)(2,1)} %up.1), custom_call_target="tpu_custom_call" | custom-call | tf_op jit(solution)/shard_map/grams/pallas_call | solution.py:281
  6.2 0.1 collective-permute-start
  6.3 2.0 %collective-permute-done.rest_0_ = s16[2320,128]{1,0:T(8,128)(2,1)S(1)} collective-permute-done((s16[2320,128]{1,0:T(8,128)(2,1)S(1)}, s16[2320,128]{1,0:T(8,128)(2,1)S(1)}, u32[]{:S(2)}, u32[]{:S(2)}) %collective-permute-start) | collective-permute-done | bytes 593952 | tf_op jit(solution)/shard_map/ppermute | solution.py:357
  8.3 0.3 %join8.1 = (f32[2,48,768]{2,1,0:T(8,128)S(1)}, s16[592,128]{1,0:T(8,128)(2,1)S(1)}, s16[592,128]{1,0:T(8,128)(2,1)S(1)}, s16[592,128]{1,0:T(8,128)(2,1)S(1)}) custom-call(f32[16,48,768]{2,1,0:T(8,128)S(1)} %get-tuple-element.13.own, s16[2320,128]{1,0:T(8,128)(2,1)S(1)} %collective-permute-done.rest_0_), custom_call_target="tpu_custom_call" | custom-call | tf_op jit(solution)/shard_map/join8/pallas_call | solution.py:333
  8.6 2.6 %collective-permute-start.1 = (s16[592,128]{1,0:T(8,128)(2,1)S(1)}, s16[592,128]{1,0:T(8,128)(2,1)S(1)}, u32[]{:S(2)}, u32[]{:S(2)}) collective-permute-start(s16[592,128]{1,0:T(8,128)(2,1)S(1)} %get-tuple-element.16), channel_id=1, source_target_pairs={{0,2},{1,9},{2,0},{3,11},{4,6},{5,13},{6,4},{7,15},{8,10},{9,1},{1... | collective-permute-start | bytes 454664 | tf_op jit(solution)/shard_map/ppermute | solution.py:362
  11.2 5.9 %collective-permute-start.2 = (s16[592,128]{1,0:T(8,128)(2,1)S(1)}, s16[592,128]{1,0:T(8,128)(2,1)S(1)}, u32[]{:S(2)}, u32[]{:S(2)}) collective-permute-start(s16[592,128]{1,0:T(8,128)(2,1)S(1)} %get-tuple-element.17), channel_id=1, source_target_pairs={{0,6},{1,3},{2,4},{3,1},{4,2},{5,7},{6,0},{7,5},{8,14},{9,11},{10,... | collective-permute-start | bytes 454664 | tf_op jit(solution)/shard_map/ppermute | solution.py:362
  17.1 0.0 collective-permute-start.3
  17.2 0.0 collective-permute-done.1.rest_0_
  17.2 4.3 %collective-permute-done.2.rest_1_ = s16[592,128]{1,0:T(8,128)(2,1)S(1)} collective-permute-done((s16[592,128]{1,0:T(8,128)(2,1)S(1)}, s16[592,128]{1,0:T(8,128)(2,1)S(1)}, u32[]{:S(2)}, u32[]{:S(2)}) %collective-permute-start.2) | collective-permute-done | bytes 151584 | tf_op jit(solution)/shard_map/ppermute | solution.py:362
  21.5 3.0 %collective-permute-done.3.rest_2_ = s16[592,128]{1,0:T(8,128)(2,1)S(1)} collective-permute-done((s16[592,128]{1,0:T(8,128)(2,1)S(1)}, s16[592,128]{1,0:T(8,128)(2,1)S(1)}, u32[]{:S(2)}, u32[]{:S(2)}) %collective-permute-start.3) | collective-permute-done | bytes 151584 | tf_op jit(solution)/shard_map/ppermute | solution.py:362
  24.5 0.2 join2.1
  24.7 2.9 %collective-permute-start.4 = (s16[304,128]{1,0:T(8,128)(2,1)S(1)}, s16[304,128]{1,0:T(8,128)(2,1)S(1)}, u32[]{:S(2)}, u32[]{:S(2)}) collective-permute-start(s16[304,128]{1,0:T(8,128)(2,1)S(1)} %get-tuple-element.20), channel_id=1, source_target_pairs={{0,8},{1,5},{2,10},{3,7},{4,12},{5,1},{6,14},{7,3},{8,0},{9,13},{1... | collective-permute-start | bytes 233480 | tf_op jit(solution)/shard_map/ppermute | solution.py:362
  27.6 2.5 %collective-permute-done.4.rest_0_ = s16[304,128]{1,0:T(8,128)(2,1)S(1)} collective-permute-done((s16[304,128]{1,0:T(8,128)(2,1)S(1)}, s16[304,128]{1,0:T(8,128)(2,1)S(1)}, u32[]{:S(2)}, u32[]{:S(2)}) %collective-permute-start.4) | collective-permute-done | bytes 77856 | tf_op jit(solution)/shard_map/ppermute | solution.py:362
  30.1 0.7 %join1.1 = f32[48,768]{1,0:T(8,128)} custom-call(f32[1,48,768]{2,1,0:T(8,128)S(1)} %get-tuple-element.19.own, s16[304,128]{1,0:T(8,128)(2,1)S(1)} %collective-permute-done.4.rest_0_), custom_call_target="tpu_custom_call" | custom-call | tf_op jit(solution)/shard_map/join1/pallas_call | solution.py:333
Async XLA Ops:
  6.2 2.1 %collective-permute-start = (s16[2320,128]{1,0:T(8,128)(2,1)S(1)}, s16[2320,128]{1,0:T(8,128)(2,1)S(1)}, u32[]{:S(2)}, u32[]{:S(2)}) collective-permute-start(s16[2320,128]{1,0:T(8,128)(2,1)S(1)} %get-tuple-element.14), channel_id=1, source_target_pairs={{0,1},{1,0},{2,3},{3,2},{4,5},{5,4},{6,7},{7,6},{8,9},{9,8},{10,11... | collective-permute-start | bytes 1781768 | tf_op jit(solution)/shard_map/ppermute | solution.py:357
  8.6 8.6 %collective-permute-start.1 = (s16[592,128]{1,0:T(8,128)(2,1)S(1)}, s16[592,128]{1,0:T(8,128)(2,1)S(1)}, u32[]{:S(2)}, u32[]{:S(2)}) collective-permute-start(s16[592,128]{1,0:T(8,128)(2,1)S(1)} %get-tuple-element.16), channel_id=1, source_target_pairs={{0,2},{1,9},{2,0},{3,11},{4,6},{5,13},{6,4},{7,15},{8,10},{9,1},{1... | collective-permute-start | bytes 454664 | tf_op jit(solution)/shard_map/ppermute | solution.py:362
  11.2 10.3 %collective-permute-start.2 = (s16[592,128]{1,0:T(8,128)(2,1)S(1)}, s16[592,128]{1,0:T(8,128)(2,1)S(1)}, u32[]{:S(2)}, u32[]{:S(2)}) collective-permute-start(s16[592,128]{1,0:T(8,128)(2,1)S(1)} %get-tuple-element.17), channel_id=1, source_target_pairs={{0,6},{1,3},{2,4},{3,1},{4,2},{5,7},{6,0},{7,5},{8,14},{9,11},{10,... | collective-permute-start | bytes 454664 | tf_op jit(solution)/shard_map/ppermute | solution.py:362
  17.1 7.4 %collective-permute-start.3 = (s16[592,128]{1,0:T(8,128)(2,1)S(1)}, s16[592,128]{1,0:T(8,128)(2,1)S(1)}, u32[]{:S(2)}, u32[]{:S(2)}) collective-permute-start(s16[592,128]{1,0:T(8,128)(2,1)S(1)} %get-tuple-element.18), channel_id=1, source_target_pairs={{0,4},{1,11},{2,6},{3,9},{4,0},{5,15},{6,2},{7,13},{8,12},{9,3},{1... | collective-permute-start | bytes 454664 | tf_op jit(solution)/shard_map/ppermute | solution.py:362
  24.7 5.4 %collective-permute-start.4 = (s16[304,128]{1,0:T(8,128)(2,1)S(1)}, s16[304,128]{1,0:T(8,128)(2,1)S(1)}, u32[]{:S(2)}, u32[]{:S(2)}) collective-permute-start(s16[304,128]{1,0:T(8,128)(2,1)S(1)} %get-tuple-element.20), channel_id=1, source_target_pairs={{0,8},{1,5},{2,10},{3,7},{4,12},{5,1},{6,14},{7,3},{8,0},{9,13},{1... | collective-permute-start | bytes 233480 | tf_op jit(solution)/shard_map/ppermute | solution.py:362
